TPU v7x, 128 devices: a whole 4x4x4 slice. The times are simulated.
128 devices in a mesh: row: 16 (over x_hi, y, core), col: 8 (over x_lo, z).
Axes of the slice: x: 4 (x_hi: 2, x_lo: 2; x = x_hi * 2 + x_lo), y: 4, z: 4, core: 2. Of those that a mesh axis runs over, the one named last changes fastest.
Arguments:
- tokens: bfloat16 [512, 512, 384], P('row', 'col'), may hold values from -6 to 6
- w_expand: bfloat16 [384, 1536], replicated, may hold values from -0.3125 to 0.3125
- b_expand: float32 [1536], replicated, may hold values from -3 to 3
- w_depth: float32 [9, 1536], replicated, may hold values from -2 to 2
- b_depth: float32 [1536], replicated, may hold values from -3 to 3
- w_project: bfloat16 [1536, 384], replicated, may hold values from -0.15625 to 0.15625
- w_qkv: bfloat16 [384, 1152], replicated, may hold values from -0.3125 to 0.3125
- w_out: bfloat16 [384, 384], replicated, may hold values from -0.3125 to 0.3125
- pos_table: float32 [12, 225], replicated, may hold values from -3.5 to 320
Outputs:
- mixed: bfloat16 [512, 512, 384], P('row', 'col')
All inputs are finite; a program needn't handle non-finite values.
Results may differ from a plain program's by a relative error of at most 0.0065.
Values may be sent and summed in bfloat16 or wider, within the bound.
A program may use at most 128 MiB of HBM per device.

v0:
```python
import functools
import math

import jax
import jax.numpy as jnp
from jax import lax
from jax.experimental import pallas as pl
from jax.experimental.pallas import tpu as pltpu
from jax.sharding import PartitionSpec as P

BF = jnp.bfloat16
F32 = jnp.float32
MESH = pl.DeviceIdType.MESH
D, FF, HEADS, GRID = 384, 1536, 12, 8
C0 = 0.7978845608
C1 = C0 * 0.044715
ALPHA = C1 ** (1.0 / 3.0)
BETA = C0 / ALPHA
LOG2E = 1.4426950408889634
NT = (((1,), (1,)), ((), ()))
TN = (((0,), (0,)), ((), ()))


def dot(a, b):
    return jnp.dot(a, b, preferred_element_type=F32)


def dot_of(a, b, dims):
    return lax.dot_general(a, b, dims, preferred_element_type=F32)


def iota(shape, dim):
    return lax.broadcasted_iota(jnp.int32, shape, dim)


def one_hot(mask):
    return mask.astype(F32).astype(BF)


def swap_8x8():
    p, n = iota((256, 256), 0), iota((256, 256), 1)
    return one_hot(n == (p // 64) * 64 + (p % 8) * 8 + (p // 8) % 8)


def swap_16x16():
    p, n = iota((256, 256), 0), iota((256, 256), 1)
    return one_hot(n == (p % 16) * 16 + p // 16)


def twice_gelu(v):
    t = jnp.tanh(v * (C0 + C1 * (v * v)))
    return v + v * t


def scaled_gelu(z):
    t = jnp.tanh(z * (z * z + BETA))
    return z + z * t


def set_taps(wd, bd, taps):
    for k in range(9):
        taps[k] = jnp.broadcast_to(wd[k : k + 1, :] * (0.5 * ALPHA), (8, FF))
    taps[9] = jnp.broadcast_to(bd[...] * ALPHA, (8, FF))


def permute_rows(tok, swap, perm, first, count):
    def step(c, _):
        x = tok[pl.ds(c * 4, 4)].reshape(256, D)
        perm[pl.ds(c * 4 + 1, 4)] = dot(swap, x).astype(BF).reshape(4, 4, 16, D)
        return 0

    lax.fori_loop(first, first + count, step, 0)


def expand_rows(perm, we, be, grown, r0, n):
    x = perm[pl.ds(r0, n)].reshape(n * 64, D)
    for b in range(6):
        sl = slice(b * 256, b * 256 + 256)
        g = twice_gelu(dot(x, we[:, sl]) + be[:, sl]).reshape(n, 8, 8, 256)
        grown[pl.ds(r0, n), 1:9, :, sl] = g
        for y in range(n):
            grown[r0 + y, 0, :, sl] = pltpu.roll(g[y, 7], 1, 0)
            grown[r0 + y, 9, :, sl] = pltpu.roll(g[y, 0], 7, 0)


def expand_sides(cells, we, be, sides, row, col, rows_last, cols_last):
    ri = iota((80, 1), 0)
    left = (col > 0).astype(F32)
    right = (col < cols_last).astype(F32)
    top = (row > 0).astype(F32)
    bottom = (row < rows_last).astype(F32)
    at = ri % 40
    keep = jnp.where(ri < 40, left, right)
    keep = keep * jnp.where(at == 32, top, 1.0) * jnp.where(at == 33, bottom, 1.0)
    for b in range(6):
        sl = slice(b * 256, b * 256 + 256)
        sides[:, sl] = twice_gelu(dot(cells, we[:, sl]) + be[:, sl]) * keep


def place_sides(sides, grown):
    def step(y, _):
        grown[y + 1, 0, 0:1, :] = sides[pl.ds(y, 1), :]
        grown[y + 1, 9, 7:8, :] = sides[pl.ds(40 + y, 1), :]
        return 0

    lax.fori_loop(0, 32, step, 0)
    for r, at in ((0, 32), (33, 33)):
        grown[r, 0, 0:1, :] = sides[at : at + 1, :]
        grown[r, 9, 7:8, :] = sides[40 + at : 41 + at, :]


def conv_project(perm, grown, taps, wp, out, r0):
    total = None
    for b in range(6):
        parts = []
        for l in range(2):
            sl = slice(b * 256 + l * 128, b * 256 + l * 128 + 128)
            w = [taps[k, :, sl] for k in range(10)]
            done = [[None] * 8 for _ in range(4)]
            for half in range(2):
                sums = [[None] * 4 for _ in range(4)]
                for rr in range(6):
                    e = [grown[r0 + rr, half * 4 + q, :, sl] for q in range(6)]
                    for p in range(3):
                        y = rr - p
                        if not 0 <= y < 4:
                            continue
                        for t in range(4):
                            s = sums[y][t]
                            for q in range(3):
                                m = e[t + q] * w[p * 3 + q]
                                s = w[9] + m if s is None else s + m
                            sums[y][t] = s
                    if rr >= 2:
                        for t in range(4):
                            done[rr - 2][half * 4 + t] = scaled_gelu(sums[rr - 2][t])
            parts.append(jnp.concatenate(sum(done, []), axis=0).astype(BF))
        a = jnp.concatenate(parts, axis=1)
        d = dot(a, wp[b * 256 : b * 256 + 256, :])
        total = d if total is None else total + d
    m = perm[pl.ds(r0 + 1, 4)].reshape(256, D).astype(F32) + total * (0.5 / ALPHA)
    out[pl.ds(r0, 4)] = m.astype(BF).reshape(4, 4, 16, D)


def build_bias(pos, shifts, bias):
    table = jnp.concatenate([pos[...], jnp.zeros((12, 31), F32)], axis=1) * LOG2E
    hi = table.astype(BF)
    rest = table - hi.astype(F32)
    mid = rest.astype(BF)
    low = (rest - mid.astype(F32)).astype(BF)
    c, lane = iota((256, 128), 0), iota((256, 128), 1)
    for js in range(8):
        pick = one_hot(c == (lane // 8) * 15 + lane % 8 - js + 7)
        shifts[:, js, :] = dot(hi, pick) + dot(mid, pick) + dot(low, pick)
    low_half = iota((8, 128), 1) < 64
    for h in range(HEADS):
        x = shifts[h]
        for i in range(8):
            a = pltpu.roll(x, (128 - (7 - i) * 8) % 128, 1)
            b = pltpu.roll(x, (64 + 128 - (7 - i) * 8) % 128, 1)
            bias[h, i * 8 : i * 8 + 8, :] = jnp.where(low_half, a, b)


def group_rows(landed, swap, grouped, normed, sb):
    x = landed[pl.ds(sb * 16, 16)].reshape(256, D)
    v = dot(swap, x)
    grouped[:, pl.ds(sb * 16, 16), :] = v.astype(BF).reshape(16, 16, D)
    centred = v - jnp.mean(v, axis=-1, keepdims=True)
    spread = jnp.mean(centred * centred, axis=-1, keepdims=True)
    y = centred * lax.rsqrt(spread + 1e-05)
    normed[:, pl.ds(sb * 16, 16), :] = y.astype(BF).reshape(16, 16, D)


def project_qkv(normed, wqkv, wvt, qk, vt):
    for c in range(4):
        x = normed[c * 4 : c * 4 + 4].reshape(256, D)
        qk[c * 256 : c * 256 + 256, :] = dot(x, wqkv[:, :768]).astype(BF)
        vt[:, c * 256 : c * 256 + 256] = dot_of(wvt[...], x, NT).astype(BF)


def attend_pair(qk, vt, bias, ctx, at):
    row = iota((256, 128), 0)
    lane = iota((256, 128), 1)
    head_mask = one_hot(row // 64 == lane // 32)
    lo = one_hot(iota((32, 128), 1) < 64)
    hi = one_hot(iota((32, 128), 1) >= 64)
    low_lanes = iota((128, 128), 1) < 64
    none = jnp.zeros((64, 128), BF)
    nothing = jnp.zeros((32, 128), BF)
    scale = LOG2E / math.sqrt(32.0)
    for b in range(3):
        q = qk[pl.ds(at, 128), b * 128 : b * 128 + 128]
        k = qk[pl.ds(at, 128), D + b * 128 : D + b * 128 + 128]
        spread_k = jnp.concatenate(
            [jnp.concatenate([k[g * 64 : g * 64 + 64]] * 4, axis=0) * head_mask for g in range(2)],
            axis=1,
        )
        spread_q = jnp.concatenate(
            [
                jnp.concatenate([q[:64], none], axis=1),
                jnp.concatenate([none, q[64:]], axis=1),
            ],
            axis=0,
        )
        scores = dot_of(spread_k, spread_q, NT)
        weights, inverse = [], []
        for h in range(4):
            s = scores[h * 64 : h * 64 + 64] * scale + bias[b * 4 + h]
            w = jnp.exp2(s - jnp.max(s, axis=0, keepdims=True))
            total = jnp.sum(w, axis=0, keepdims=True)
            inverse.append(jnp.broadcast_to(1.0 / total, (32, 128)))
            weights.append(w.astype(BF))
        weights = jnp.concatenate(weights, axis=0)
        x = vt[b * 128 : b * 128 + 128, pl.ds(at, 128)]
        y = jnp.concatenate([x[:, 64:], x[:, :64]], axis=1)
        rows = []
        for first, second in ((x, y), (y, x)):
            rows.append(jnp.concatenate([first[0:32] * lo, nothing], axis=1))
            rows.append(jnp.concatenate([second[32:64] * hi, nothing], axis=1))
            rows.append(jnp.concatenate([nothing, first[64:96] * lo], axis=1))
            rows.append(jnp.concatenate([nothing, second[96:128] * hi], axis=1))
        both = dot(jnp.concatenate(rows, axis=0), weights)
        mine = jnp.where(low_lanes, both[:128], both[128:])
        mine = mine * jnp.concatenate(inverse, axis=0)
        ctx[b * 128 : b * 128 + 128, pl.ds(at, 128)] = mine.astype(BF)


def project_out(ctx, wout, grouped):
    for c in range(4):
        d = dot_of(ctx[:, c * 256 : c * 256 + 256], wout[...], TN)
        m = grouped[c * 4 : c * 4 + 4].reshape(256, D).astype(F32) + d
        grouped[c * 4 : c * 4 + 4] = m.astype(BF).reshape(4, 64, D)


def ungroup_rows(grouped, swap, out, sb):
    x = grouped[:, pl.ds(sb * 16, 16), :].reshape(256, D)
    out[pl.ds(sb * 16, 16)] = dot(swap, x).astype(BF).reshape(16, 16, D)


def place():
    row, col = lax.axis_index("row"), lax.axis_index("col")
    x = (row // 8) * 2 + col // 4
    return row % 2, x, (row // 2) % 4, col % 4


def device(core, x, y, z):
    return ((x // 2) * 8 + y * 2 + core, (x % 2) * 4 + z)


def slot(x, y, z):
    return ((x // 2) * 4 + y) * 8 + (x % 2) * 4 + z


def mbconv_kernel(tok, rows, cells, we, be, wd, bd, wp, out, perm, grown, sides, taps):
    row, col = lax.axis_index("row"), lax.axis_index("col")
    swap = swap_8x8()
    permute_rows(tok, swap, perm, 0, 8)
    ends = dot(swap[:128, :128], rows[...].reshape(128, D)).astype(BF).reshape(2, 4, 16, D)
    perm[0] = ends[0]
    perm[33] = ends[1]
    set_taps(wd, bd, taps)

    def grow(c, _):
        expand_rows(perm, we, be, grown, c * 4 + 1, 4)
        return 0

    lax.fori_loop(0, 8, grow, 0)
    expand_rows(perm, we, be, grown, 0, 1)
    expand_rows(perm, we, be, grown, 33, 1)

    @pl.when(row == 0)
    def _():
        grown[0] = jnp.zeros(grown.shape[1:], F32)

    @pl.when(row == 15)
    def _():
        grown[33] = jnp.zeros(grown.shape[1:], F32)

    expand_sides(cells[...], we, be, sides, row, col, 15, 7)
    place_sides(sides, grown)

    def mix(c, _):
        conv_project(perm, grown, taps, wp, out, c * 4)
        return 0

    lax.fori_loop(0, 8, mix, 0)


def attention_kernel(landed, wqkv, wout, pos, out, shifts, bias, wvt, grouped, normed, qk, vt, ctx):
    build_bias(pos, shifts, bias)
    eye = one_hot(iota((D, D), 0) == iota((D, D), 1))
    wvt[...] = dot_of(eye, wqkv[:, 768:], NT).astype(BF)
    swap = swap_16x16()
    for h in range(2):
        for sb in range(4):
            group_rows(landed.at[h], swap, grouped, normed, sb)
        project_qkv(normed, wqkv, wvt, qk, vt)

        def pair(n, _):
            attend_pair(qk, vt, bias, ctx, pl.multiple_of(n * 128, 128))
            return 0

        lax.fori_loop(0, 8, pair, 0)
        project_out(ctx, wout, grouped)
        for sb in range(4):
            ungroup_rows(grouped, swap, out.at[h], sb)


OFFSETS = [(a, b, c) for a in (2, 1, 3, 0) for b in (2, 1, 3, 0) for c in (2, 1, 3, 0)][:63]


def exchange_kernel(back, source, out, send_sem, recv_sem, own_sem):
    core, x, y, z = place()
    barrier = pltpu.get_barrier_semaphore()
    for dx, dy, dz in OFFSETS:
        to = device(core, (x + dx) % 4, (y + dy) % 4, (z + dz) % 4)
        pl.semaphore_signal(barrier, inc=1, device_id=to, device_id_type=MESH)
    pl.semaphore_wait(barrier, 63)
    me = slot(x, y, z)

    def ends(h, X, Y, Z):
        if back:
            return source.at[h, slot(X, Y, Z)], out.at[16 * h + 4 * ((x + y + z) % 4) + y, z]
        return source.at[16 * h + 4 * ((X + Y + Z) % 4) + Y, Z], out.at[h, me]

    copies = []
    for h in range(2):
        for n, (dx, dy, dz) in enumerate(OFFSETS):
            X, Y, Z = (x + dx) % 4, (y + dy) % 4, (z + dz) % 4
            src, dst = ends(h, X, Y, Z)
            copy = pltpu.make_async_remote_copy(
                src, dst, send_sem.at[h, n], recv_sem.at[h, n],
                device_id=device(core, X, Y, Z), device_id_type=MESH,
            )
            copy.start()
            copies.append(copy)
        own = pltpu.make_async_copy(*ends(h, x, y, z), own_sem.at[h])
        own.start()
        copies.append(own)
    for copy in copies:
        copy.wait()


def natural_kernel(x, out):
    swap = swap_8x8()

    def step(c, _):
        v = dot(swap, x[pl.ds(c * 4, 4)].reshape(256, D))
        out[pl.ds(c * 4, 4)] = v.astype(BF).reshape(4, 64, D)
        return 0

    lax.fori_loop(0, 8, step, 0)


VM = pl.BlockSpec(memory_space=pltpu.VMEM)
BIG = 58 << 20


def exchange(back, source, shape):
    return pl.pallas_call(
        functools.partial(exchange_kernel, back),
        out_shape=jax.ShapeDtypeStruct(shape, BF),
        in_specs=[VM],
        out_specs=VM,
        scratch_shapes=[
            pltpu.SemaphoreType.DMA((2, 63)),
            pltpu.SemaphoreType.DMA((2, 63)),
            pltpu.SemaphoreType.DMA((2,)),
        ],
        compiler_params=pltpu.CompilerParams(
            collective_id=1 if back else 0, has_side_effects=True, vmem_limit_bytes=BIG
        ),
    )(source)


def shifted(x, axis, step):
    size = lax.axis_size(axis)
    return lax.ppermute(x, axis, [(i, i + step) for i in range(size) if 0 <= i + step < size])


def on_device(tokens, we, be, wd, bd, wp, wqkv, wout, pos):
    top = shifted(tokens[31], "row", 1)
    bottom = shifted(tokens[0], "row", -1)
    rim = lambda c: jnp.concatenate([tokens[:, c], top[c][None], bottom[c][None]], axis=0)
    left = shifted(rim(63), "col", 1)
    right = shifted(rim(0), "col", -1)
    blank = jnp.zeros((6, D), BF)
    cells = jnp.concatenate([left, blank, right, blank], axis=0)
    mb = pl.pallas_call(
        mbconv_kernel,
        out_shape=jax.ShapeDtypeStruct((32, 4, 16, D), BF),
        in_specs=[VM] * 8,
        out_specs=VM,
        scratch_shapes=[
            pltpu.VMEM((34, 4, 16, D), BF),
            pltpu.VMEM((34, 10, 8, FF), F32),
            pltpu.VMEM((80, FF), F32),
            pltpu.VMEM((10, 8, FF), F32),
        ],
        compiler_params=pltpu.CompilerParams(vmem_limit_bytes=BIG),
    )(tokens, jnp.stack([top, bottom]), cells, we, be.reshape(1, FF), wd, bd.reshape(1, FF), wp)
    landed = exchange(False, mb, (2, 64, 16, D))
    result = pl.pallas_call(
        attention_kernel,
        out_shape=jax.ShapeDtypeStruct((2, 64, 16, D), BF),
        in_specs=[VM] * 4,
        out_specs=VM,
        scratch_shapes=[
            pltpu.VMEM((12, 8, 128), F32),
            pltpu.VMEM((12, 64, 128), F32),
            pltpu.VMEM((D, D), BF),
            pltpu.VMEM((16, 64, D), BF),
            pltpu.VMEM((16, 64, D), BF),
            pltpu.VMEM((1024, 768), BF),
            pltpu.VMEM((D, 1024), BF),
            pltpu.VMEM((D, 1024), BF),
        ],
        compiler_params=pltpu.CompilerParams(vmem_limit_bytes=BIG),
    )(landed, wqkv, wout, pos)
    returned = exchange(True, result, (32, 4, 16, D))
    return pl.pallas_call(
        natural_kernel,
        out_shape=jax.ShapeDtypeStruct((32, 64, D), BF),
        in_specs=[VM],
        out_specs=VM,
        compiler_params=pltpu.CompilerParams(vmem_limit_bytes=BIG),
    )(returned)


def solution(mesh):
    placed = (P("row", "col", None), P(), P(), P(), P(), P(), P(), P(), P())
    return jax.shard_map(
        on_device, mesh=mesh, in_specs=placed, out_specs=P("row", "col", None), check_vma=False
    )
```

profile of v0, /device:TPU:1, one launch (start us, length us, event | category | flops | bytes accessed | tf_op | source)
XLA Modules:
  0.0 139.6 jit_solution(5620972712901553956)
XLA Ops:
  0.0 0.8 slice_bitcast_fusion.1
  0.8 4.6 %collective-permute-start = (bf16[64,384]{1,0:T(8,128)(2,1)S(1)}, bf16[64,384]{1,0:T(8,128)(2,1)S(1)}, u32[]{:S(2)}, u32[]{:S(2)}) collective-permute-start(bf16[64,384]{1,0:T(8,128)(2,1)S(1)} %get-tuple-element.7), channel_id=1, source_target_pairs={{0,8},{8,16},{16,24},{24,32},{32,40},{40,48},{48,56},{56,64},{64,7... | collective-permute-start | bytes 147464 | tf_op jit(solution)/shard_map/ppermute | solution.py:378
  5.4 1.9 %collective-permute-start.1 = (bf16[64,384]{1,0:T(8,128)(2,1)S(1)}, bf16[64,384]{1,0:T(8,128)(2,1)S(1)}, u32[]{:S(2)}, u32[]{:S(2)}) collective-permute-start(bf16[64,384]{1,0:T(8,128)(2,1)S(1)} %get-tuple-element.8), channel_id=1, source_target_pairs={{8,0},{16,8},{24,16},{32,24},{40,32},{48,40},{56,48},{64,56},{72,6... | collective-permute-start | bytes 147464 | tf_op jit(solution)/shard_map/ppermute | solution.py:378
  7.4 1.1 fusion
  8.5 1.3 reshape.6.be
  9.8 1.3 reshape.7.bd
  11.1 0.0 collective-permute-done
  11.1 0.0 collective-permute-done.1
  11.2 1.3 collective-permute-start.3
  12.5 4.2 %collective-permute-start.2 = (bf16[34,384]{1,0:T(8,128)(2,1)S(1)}, bf16[34,384]{1,0:T(8,128)(2,1)S(1)}, u32[]{:S(2)}, u32[]{:S(2)}) collective-permute-start(bf16[34,384]{1,0:T(8,128)(2,1)S(1)} %pad_maximum_fusion.2), channel_id=1, source_target_pairs={{0,1},{1,2},{2,3},{3,4},{4,5},{5,6},{6,7},{8,9},{9,10},{10,11},{11... | collective-permute-start | bytes 78344 | tf_op jit(solution)/shard_map/ppermute | solution.py:378
  16.7 0.6 pad_maximum_fusion.rows
  17.3 0.0 collective-permute-done.3
  17.3 0.3 collective-permute-done.2
  17.7 0.6 pad_maximum_fusion.1.cells
  18.3 25.4 %shard_map.91.source = bf16[32,4,16,384]{3,2,1,0:T(8,128)(2,1)} custom-call(bf16[32,64,384]{2,1,0:T(8,128)(2,1)} %tok.1, bf16[2,64,384]{2,1,0:T(8,128)(2,1)} %pad_maximum_fusion.rows, bf16[80,384]{1,0:T(8,128)(2,1)} %pad_maximum_fusion.1.cells, bf16[384,1536]{1,0:T(8,128)(2,1)} %we.1, f32[1,1536]{1,0:T(1,128)} %reshape.6.be, f32[9,1536]{1,0:T(8,128)} %wd.1, ...), custom_call_target="tpu_custom_call" | custom-call | tf_op jit(solution)/shard_map/pallas_call | solution.py:389
  43.7 40.9 %shard_map.92.landed = bf16[2,64,16,384]{3,2,1,0:T(8,128)(2,1)} custom-call(bf16[32,4,16,384]{3,2,1,0:T(8,128)(2,1)} %shard_map.91.source), custom_call_target="tpu_custom_call" | custom-call | tf_op jit(solution)/shard_map/pallas_call | solution.py:360
  84.6 21.5 %shard_map.93.source = bf16[2,64,16,384]{3,2,1,0:T(8,128)(2,1)} custom-call(bf16[2,64,16,384]{3,2,1,0:T(8,128)(2,1)} %shard_map.92.landed, bf16[384,1152]{1,0:T(8,128)(2,1)} %wqkv.1, bf16[384,384]{1,0:T(8,128)(2,1)} %wout.1, f32[12,225]{1,0:T(8,128)} %pos.1), custom_call_target="tpu_custom_call" | custom-call | tf_op jit(solution)/shard_map/pallas_call | solution.py:403
  106.1 29.1 %shard_map.94.x = bf16[32,4,16,384]{3,2,1,0:T(8,128)(2,1)} custom-call(bf16[2,64,16,384]{3,2,1,0:T(8,128)(2,1)} %shard_map.93.source), custom_call_target="tpu_custom_call" | custom-call | tf_op jit(solution)/shard_map/pallas_call | solution.py:360
  135.2 4.4 %shard_map.95 = bf16[32,64,384]{2,1,0:T(8,128)(2,1)} custom-call(bf16[32,4,16,384]{3,2,1,0:T(8,128)(2,1)} %shard_map.94.x), custom_call_target="tpu_custom_call" | custom-call | tf_op jit(solution)/shard_map/pallas_call | solution.py:421
  (7 shorter events, 0.1 us)
Async XLA Ops:
  0.8 10.3 %collective-permute-start = (bf16[64,384]{1,0:T(8,128)(2,1)S(1)}, bf16[64,384]{1,0:T(8,128)(2,1)S(1)}, u32[]{:S(2)}, u32[]{:S(2)}) collective-permute-start(bf16[64,384]{1,0:T(8,128)(2,1)S(1)} %get-tuple-element.7), channel_id=1, source_target_pairs={{0,8},{8,16},{16,24},{24,32},{32,40},{40,48},{48,56},{56,64},{64,7... | collective-permute-start | bytes 147464 | tf_op jit(solution)/shard_map/ppermute | solution.py:378
  5.4 5.7 %collective-permute-start.1 = (bf16[64,384]{1,0:T(8,128)(2,1)S(1)}, bf16[64,384]{1,0:T(8,128)(2,1)S(1)}, u32[]{:S(2)}, u32[]{:S(2)}) collective-permute-start(bf16[64,384]{1,0:T(8,128)(2,1)S(1)} %get-tuple-element.8), channel_id=1, source_target_pairs={{8,0},{16,8},{24,16},{32,24},{40,32},{48,40},{56,48},{64,56},{72,6... | collective-permute-start | bytes 147464 | tf_op jit(solution)/shard_map/ppermute | solution.py:378
  11.2 6.2 %collective-permute-start.3 = (bf16[34,384]{1,0:T(8,128)(2,1)S(1)}, bf16[34,384]{1,0:T(8,128)(2,1)S(1)}, u32[]{:S(2)}, u32[]{:S(2)}) collective-permute-start(bf16[34,384]{1,0:T(8,128)(2,1)S(1)} %pad_maximum_fusion.3), channel_id=1, source_target_pairs={{1,0},{2,1},{3,2},{4,3},{5,4},{6,5},{7,6},{9,8},{10,9},{11,10},{12... | collective-permute-start | bytes 78344 | tf_op jit(solution)/shard_map/ppermute | solution.py:378
  12.5 5.2 %collective-permute-start.2 = (bf16[34,384]{1,0:T(8,128)(2,1)S(1)}, bf16[34,384]{1,0:T(8,128)(2,1)S(1)}, u32[]{:S(2)}, u32[]{:S(2)}) collective-permute-start(bf16[34,384]{1,0:T(8,128)(2,1)S(1)} %pad_maximum_fusion.2), channel_id=1, source_target_pairs={{0,1},{1,2},{2,3},{3,4},{4,5},{5,6},{6,7},{8,9},{9,10},{10,11},{11... | collective-permute-start | bytes 78344 | tf_op jit(solution)/shard_map/ppermute | solution.py:378
where the time goes:
time: 140 us
  Pallas kernels  121 us (86%)
  starting transfers between devices  12 us (9%)
  local copies, waits for them, and re-layouts  4.57 us (3%)
    pallas_call x2, Pallas kernels, exchange(): pl.pallas_call(functools.partial(exchange_kernel, back), out_shape=jax.Sh...  70 us
    pallas_call x1, Pallas kernels, on_device(): pl.pallas_call(mbconv_kernel, out_shape=jax.ShapeDtypeStruct((32, 4, 16,...  25.4 us
    pallas_call x1, Pallas kernels, on_device(): pl.pallas_call(attention_kernel, out_shape=jax.ShapeDtypeStruct((2, 64, 1...  21.5 us
    ppermute x4, starting transfers between devices, shifted(): lax.ppermute(x, axis, [(i, i + step) for i in range(size) if 0 <= i + ste...  12 us
    pallas_call x1, Pallas kernels, on_device(): pl.pallas_call(natural_kernel, out_shape=jax.ShapeDtypeStruct((32, 64, D)...  4.42 us
  transfers between devices with their start and end apart: 4, of which 1 were waited for; matrix products, arithmetic and copies ran while one was open for 3% of the time, Pallas kernels for 0%

commit v1 on v0

--- a/solution.py
+++ b/solution.py
@@ -63,13 +63,16 @@
     taps[9] = jnp.broadcast_to(bd[...] * ALPHA, (8, FF))
 
 
-def permute_rows(tok, swap, perm, first, count):
-    def step(c, _):
+def permute_rows(tok, swap, perm, edges):
+    r, n = iota((64, 256), 0), iota((64, 256), 1)
+
+    def step(c, total):
         x = tok[pl.ds(c * 4, 4)].reshape(256, D)
         perm[pl.ds(c * 4 + 1, 4)] = dot(swap, x).astype(BF).reshape(4, 4, 16, D)
-        return 0
-
-    lax.fori_loop(first, first + count, step, 0)
+        pick = one_hot(n == (r % 32 - 4 * c) * 64 + (r // 32) * 63)
+        return total + dot(pick, x)
+
+    edges[...] = lax.fori_loop(0, 8, step, jnp.zeros((64, D), F32)).astype(BF)
 
 
 def expand_rows(perm, we, be, grown, r0, n):
@@ -84,14 +87,14 @@
 
 
 def expand_sides(cells, we, be, sides, row, col, rows_last, cols_last):
-    ri = iota((80, 1), 0)
+    ri = iota((128, 1), 0)
     left = (col > 0).astype(F32)
     right = (col < cols_last).astype(F32)
     top = (row > 0).astype(F32)
     bottom = (row < rows_last).astype(F32)
-    at = ri % 40
-    keep = jnp.where(ri < 40, left, right)
-    keep = keep * jnp.where(at == 32, top, 1.0) * jnp.where(at == 33, bottom, 1.0)
+    side = jnp.where(ri < 64, ri // 32, (ri // 16) % 2)
+    keep = jnp.where(side == 0, left, right)
+    keep = keep * jnp.where(ri < 64, 1.0, jnp.where(ri < 96, top, bottom))
     for b in range(6):
         sl = slice(b * 256, b * 256 + 256)
         sides[:, sl] = twice_gelu(dot(cells, we[:, sl]) + be[:, sl]) * keep
@@ -100,13 +103,13 @@
 def place_sides(sides, grown):
     def step(y, _):
         grown[y + 1, 0, 0:1, :] = sides[pl.ds(y, 1), :]
-        grown[y + 1, 9, 7:8, :] = sides[pl.ds(40 + y, 1), :]
+        grown[y + 1, 9, 7:8, :] = sides[pl.ds(32 + y, 1), :]
         return 0
 
     lax.fori_loop(0, 32, step, 0)
-    for r, at in ((0, 32), (33, 33)):
-        grown[r, 0, 0:1, :] = sides[at : at + 1, :]
-        grown[r, 9, 7:8, :] = sides[40 + at : 41 + at, :]
+    for r, at in ((0, 64), (33, 96)):
+        grown[r, 0, 0:1, :] = sides[at + 15 : at + 16, :]
+        grown[r, 9, 7:8, :] = sides[at + 16 : at + 17, :]
 
 
 def conv_project(perm, grown, taps, wp, out, r0):
@@ -251,22 +254,73 @@
     return ((x // 2) * 4 + y) * 8 + (x % 2) * 4 + z
 
 
-def mbconv_kernel(tok, rows, cells, we, be, wd, bd, wp, out, perm, grown, sides, taps):
+ORDER = [(a, b, c) for a in (2, 1, 3, 0) for b in (2, 1, 3, 0) for c in (2, 1, 3, 0)]
+OFFSETS = sorted(ORDER[:63], key=lambda d: -sum(min(k, 4 - k) for k in d))
+NEAR = [(1, 0), (-1, 0), (0, 1), (0, -1), (1, 1), (1, -1), (-1, 1), (-1, -1)]
+
+
+def block_kernel(
+    tok, we, be, wd, bd, wp, wqkv, wout, pos, out,
+    perm, edges, halo, grown, sides, taps, flat, mb, landed, leaving, back,
+    shifts, bias, wvt, grouped, normed, qk, vt, ctx,
+    halo_send, halo_recv, go_send, go_recv, back_send, back_recv,
+):
     row, col = lax.axis_index("row"), lax.axis_index("col")
+    core, x, y, z = place()
+    me = slot(x, y, z)
+
+    def beside(dr, dc):
+        return (row + dr) % 16, (col + dc) % 8
+
+    barrier = pltpu.get_barrier_semaphore()
+    for dr, dc in NEAR:
+        if dr != 0:
+            pl.semaphore_signal(barrier, inc=1, device_id=beside(dr, dc), device_id_type=MESH)
+    for dx, dy, dz in OFFSETS:
+        to = device(core, (x + dx) % 4, (y + dy) % 4, (z + dz) % 4)
+        pl.semaphore_signal(barrier, inc=1, device_id=to, device_id_type=MESH)
+
     swap = swap_8x8()
-    permute_rows(tok, swap, perm, 0, 8)
-    ends = dot(swap[:128, :128], rows[...].reshape(128, D)).astype(BF).reshape(2, 4, 16, D)
+    permute_rows(tok, swap, perm, edges)
+    for k in range(12):
+        sl = slice(k * 128, k * 128 + 128)
+        flat[0:1, sl] = be[sl].reshape(1, 128)
+        flat[1:2, sl] = bd[sl].reshape(1, 128)
+    pl.semaphore_wait(barrier, 69)
+
+    rims = [
+        (tok.at[31], halo.at[0:64], (1, 0)),
+        (tok.at[0], halo.at[64:128], (-1, 0)),
+        (edges.at[32:64], halo.at[128:160], (0, 1)),
+        (edges.at[0:32], halo.at[160:192], (0, -1)),
+        (tok.at[31, 48:64], halo.at[192:208], (1, 1)),
+        (tok.at[31, 0:16], halo.at[208:224], (1, -1)),
+        (tok.at[0, 48:64], halo.at[224:240], (-1, 1)),
+        (tok.at[0, 0:16], halo.at[240:256], (-1, -1)),
+    ]
+    for src, dst, (dr, dc) in rims:
+        pltpu.make_async_remote_copy(
+            src, dst, halo_send, halo_recv, device_id=beside(dr, dc), device_id_type=MESH
+        ).start()
+
+    set_taps(wd, flat.at[1:2], taps)
+    bias_row = flat.at[0:1]
+
+    def grow(c, _):
+        expand_rows(perm, we, bias_row, grown, c * 4 + 1, 4)
+        return 0
+
+    lax.fori_loop(0, 8, grow, 0)
+    build_bias(pos, shifts, bias)
+    eye = one_hot(iota((D, D), 0) == iota((D, D), 1))
+    wvt[...] = dot_of(eye, wqkv[:, 768:], NT).astype(BF)
+
+    pltpu.make_async_copy(halo, halo, halo_recv).wait()
+    ends = dot(swap[:128, :128], halo[0:128, :]).astype(BF).reshape(2, 4, 16, D)
     perm[0] = ends[0]
     perm[33] = ends[1]
-    set_taps(wd, bd, taps)
-
-    def grow(c, _):
-        expand_rows(perm, we, be, grown, c * 4 + 1, 4)
-        return 0
-
-    lax.fori_loop(0, 8, grow, 0)
-    expand_rows(perm, we, be, grown, 0, 1)
-    expand_rows(perm, we, be, grown, 33, 1)
+    expand_rows(perm, we, bias_row, grown, 0, 1)
+    expand_rows(perm, we, bias_row, grown, 33, 1)
 
     @pl.when(row == 0)
     def _():
@@ -276,24 +330,43 @@
     def _():
         grown[33] = jnp.zeros(grown.shape[1:], F32)
 
-    expand_sides(cells[...], we, be, sides, row, col, 15, 7)
+    expand_sides(halo[128:256, :], we, bias_row, sides, row, col, 15, 7)
     place_sides(sides, grown)
 
-    def mix(c, _):
-        conv_project(perm, grown, taps, wp, out, c * 4)
+    def mix(n, _):
+        h, m = n // 4, n % 4
+        k = (x + y + z + m) % 4
+        conv_project(perm, grown, taps, wp, mb, 16 * h + 4 * k)
+        for dy, dz in [(b, c) for b in (2, 1, 3, 0) for c in (2, 1, 3, 0)]:
+            Y, Z = (y + dy) % 4, (z + dz) % 4
+            X = (k - Y - Z + 8) % 4
+            piece = mb.at[16 * h + 4 * k + Y, Z]
+
+            def send():
+                pltpu.make_async_remote_copy(
+                    piece, landed.at[h, me], go_send.at[h], go_recv.at[h],
+                    device_id=device(core, X, Y, Z), device_id_type=MESH,
+                ).start()
+
+            if (dy, dz) != (0, 0):
+                send()
+            else:
+                pl.when(m != 0)(send)
+
+                @pl.when(m == 0)
+                def _():
+                    pltpu.make_async_copy(piece, landed.at[h, me], go_recv.at[h]).start()
         return 0
 
     lax.fori_loop(0, 8, mix, 0)
 
-
-def attention_kernel(landed, wqkv, wout, pos, out, shifts, bias, wvt, grouped, normed, qk, vt, ctx):
-    build_bias(pos, shifts, bias)
-    eye = one_hot(iota((D, D), 0) == iota((D, D), 1))
-    wvt[...] = dot_of(eye, wqkv[:, 768:], NT).astype(BF)
-    swap = swap_16x16()
-    for h in range(2):
+    swap16 = swap_16x16()
+
+    def attend(h, _):
+        here = landed.at[h]
+        pltpu.make_async_copy(here, here, go_recv.at[h]).wait()
         for sb in range(4):
-            group_rows(landed.at[h], swap, grouped, normed, sb)
+            group_rows(here, swap16, grouped, normed, sb)
         project_qkv(normed, wqkv, wvt, qk, vt)
 
         def pair(n, _):
@@ -303,128 +376,57 @@
         lax.fori_loop(0, 8, pair, 0)
         project_out(ctx, wout, grouped)
         for sb in range(4):
-            ungroup_rows(grouped, swap, out.at[h], sb)
-
-
-OFFSETS = [(a, b, c) for a in (2, 1, 3, 0) for b in (2, 1, 3, 0) for c in (2, 1, 3, 0)][:63]
-
-
-def exchange_kernel(back, source, out, send_sem, recv_sem, own_sem):
-    core, x, y, z = place()
-    barrier = pltpu.get_barrier_semaphore()
-    for dx, dy, dz in OFFSETS:
-        to = device(core, (x + dx) % 4, (y + dy) % 4, (z + dz) % 4)
-        pl.semaphore_signal(barrier, inc=1, device_id=to, device_id_type=MESH)
-    pl.semaphore_wait(barrier, 63)
-    me = slot(x, y, z)
-
-    def ends(h, X, Y, Z):
-        if back:
-            return source.at[h, slot(X, Y, Z)], out.at[16 * h + 4 * ((x + y + z) % 4) + y, z]
-        return source.at[16 * h + 4 * ((X + Y + Z) % 4) + Y, Z], out.at[h, me]
-
-    copies = []
+            ungroup_rows(grouped, swap16, leaving.at[h], sb)
+        mine = back.at[16 * h + 4 * ((x + y + z) % 4) + y, z]
+        for dx, dy, dz in OFFSETS:
+            X, Y, Z = (x + dx) % 4, (y + dy) % 4, (z + dz) % 4
+            pltpu.make_async_remote_copy(
+                leaving.at[h, slot(X, Y, Z)], mine, back_send.at[h], back_recv.at[h],
+                device_id=device(core, X, Y, Z), device_id_type=MESH,
+            ).start()
+        pltpu.make_async_copy(leaving.at[h, me], mine, back_recv.at[h]).start()
+        return 0
+
+    lax.fori_loop(0, 2, attend, 0)
+
     for h in range(2):
-        for n, (dx, dy, dz) in enumerate(OFFSETS):
-            X, Y, Z = (x + dx) % 4, (y + dy) % 4, (z + dz) % 4
-            src, dst = ends(h, X, Y, Z)
-            copy = pltpu.make_async_remote_copy(
-                src, dst, send_sem.at[h, n], recv_sem.at[h, n],
-                device_id=device(core, X, Y, Z), device_id_type=MESH,
-            )
-            copy.start()
-            copies.append(copy)
-        own = pltpu.make_async_copy(*ends(h, x, y, z), own_sem.at[h])
-        own.start()
-        copies.append(own)
-    for copy in copies:
-        copy.wait()
-
-
-def natural_kernel(x, out):
-    swap = swap_8x8()
-
-    def step(c, _):
-        v = dot(swap, x[pl.ds(c * 4, 4)].reshape(256, D))
-        out[pl.ds(c * 4, 4)] = v.astype(BF).reshape(4, 64, D)
-        return 0
-
-    lax.fori_loop(0, 8, step, 0)
-
-
-VM = pl.BlockSpec(memory_space=pltpu.VMEM)
-BIG = 58 << 20
-
-
-def exchange(back, source, shape):
+        here = back.at[16 * h : 16 * h + 16]
+        pltpu.make_async_copy(here, here, back_recv.at[h]).wait()
+
+        def finish(c, _):
+            v = dot(swap, back[pl.ds(c * 4, 4)].reshape(256, D))
+            out[pl.ds(c * 4, 4)] = v.astype(BF).reshape(4, 64, D)
+            return 0
+
+        lax.fori_loop(4 * h, 4 * h + 4, finish, 0)
+    pltpu.make_async_copy(halo, halo, halo_send).wait()
+    for h in range(2):
+        sent = landed.at[h, 0:63]
+        pltpu.make_async_copy(sent, sent, go_send.at[h]).wait()
+        pltpu.make_async_copy(sent, sent, back_send.at[h]).wait()
+
+
+def on_device(tokens, we, be, wd, bd, wp, wqkv, wout, pos):
+    vm = pl.BlockSpec(memory_space=pltpu.VMEM)
+    shapes = [
+        ((34, 4, 16, D), BF), ((64, D), BF), ((256, D), BF), ((34, 10, 8, FF), F32),
+        ((128, FF), F32), ((10, 8, FF), F32), ((8, FF), F32), ((32, 4, 16, D), BF),
+        ((2, 64, 16, D), BF), ((2, 64, 16, D), BF), ((32, 4, 16, D), BF),
+        ((12, 8, 128), F32), ((12, 64, 128), F32), ((D, D), BF), ((16, 64, D), BF),
+        ((16, 64, D), BF), ((1024, 768), BF), ((D, 1024), BF), ((D, 1024), BF),
+    ]
+    dma = pltpu.SemaphoreType.DMA
     return pl.pallas_call(
-        functools.partial(exchange_kernel, back),
-        out_shape=jax.ShapeDtypeStruct(shape, BF),
-        in_specs=[VM],
-        out_specs=VM,
-        scratch_shapes=[
-            pltpu.SemaphoreType.DMA((2, 63)),
-            pltpu.SemaphoreType.DMA((2, 63)),
-            pltpu.SemaphoreType.DMA((2,)),
-        ],
+        block_kernel,
+        out_shape=jax.ShapeDtypeStruct((32, 64, D), BF),
+        in_specs=[vm] * 9,
+        out_specs=vm,
+        scratch_shapes=[pltpu.VMEM(*s) for s in shapes]
+        + [dma, dma, dma((2,)), dma((2,)), dma((2,)), dma((2,))],
         compiler_params=pltpu.CompilerParams(
-            collective_id=1 if back else 0, has_side_effects=True, vmem_limit_bytes=BIG
+            collective_id=0, has_side_effects=True, vmem_limit_bytes=58 << 20
         ),
-    )(source)
-
-
-def shifted(x, axis, step):
-    size = lax.axis_size(axis)
-    return lax.ppermute(x, axis, [(i, i + step) for i in range(size) if 0 <= i + step < size])
-
-
-def on_device(tokens, we, be, wd, bd, wp, wqkv, wout, pos):
-    top = shifted(tokens[31], "row", 1)
-    bottom = shifted(tokens[0], "row", -1)
-    rim = lambda c: jnp.concatenate([tokens[:, c], top[c][None], bottom[c][None]], axis=0)
-    left = shifted(rim(63), "col", 1)
-    right = shifted(rim(0), "col", -1)
-    blank = jnp.zeros((6, D), BF)
-    cells = jnp.concatenate([left, blank, right, blank], axis=0)
-    mb = pl.pallas_call(
-        mbconv_kernel,
-        out_shape=jax.ShapeDtypeStruct((32, 4, 16, D), BF),
-        in_specs=[VM] * 8,
-        out_specs=VM,
-        scratch_shapes=[
-            pltpu.VMEM((34, 4, 16, D), BF),
-            pltpu.VMEM((34, 10, 8, FF), F32),
-            pltpu.VMEM((80, FF), F32),
-            pltpu.VMEM((10, 8, FF), F32),
-        ],
-        compiler_params=pltpu.CompilerParams(vmem_limit_bytes=BIG),
-    )(tokens, jnp.stack([top, bottom]), cells, we, be.reshape(1, FF), wd, bd.reshape(1, FF), wp)
-    landed = exchange(False, mb, (2, 64, 16, D))
-    result = pl.pallas_call(
-        attention_kernel,
-        out_shape=jax.ShapeDtypeStruct((2, 64, 16, D), BF),
-        in_specs=[VM] * 4,
-        out_specs=VM,
-        scratch_shapes=[
-            pltpu.VMEM((12, 8, 128), F32),
-            pltpu.VMEM((12, 64, 128), F32),
-            pltpu.VMEM((D, D), BF),
-            pltpu.VMEM((16, 64, D), BF),
-            pltpu.VMEM((16, 64, D), BF),
-            pltpu.VMEM((1024, 768), BF),
-            pltpu.VMEM((D, 1024), BF),
-            pltpu.VMEM((D, 1024), BF),
-        ],
-        compiler_params=pltpu.CompilerParams(vmem_limit_bytes=BIG),
-    )(landed, wqkv, wout, pos)
-    returned = exchange(True, result, (32, 4, 16, D))
-    return pl.pallas_call(
-        natural_kernel,
-        out_shape=jax.ShapeDtypeStruct((32, 64, D), BF),
-        in_specs=[VM],
-        out_specs=VM,
-        compiler_params=pltpu.CompilerParams(vmem_limit_bytes=BIG),
-    )(returned)
+    )(tokens, we, be, wd, bd, wp, wqkv, wout, pos)
 
 
 def solution(mesh):

time: 140 us -> 70.2 us (0.50)
  Pallas kernels: 121 us -> 67.3 us
  starting transfers between devices: 12 us -> 0 us
  local copies, waits for them, and re-layouts: 4.57 us -> 2.71 us
    pallas_call x5 -> x1, Pallas kernels: 121 us -> 67.3 us  [on_device(): pl.pallas_call(block_kernel, out_shape=jax.ShapeDtypeStruct((32, 64, D),...]
    ppermute x4 -> x0, starting transfers between devices: 12 us -> none  [shifted(): lax.ppermute(x, axis, [(i, i + step) for i in range(size) if 0 <= i + ste...]
    unnamed x2 -> x1, local copies, waits for them, and re-layouts: 0.01 us -> 2.71 us
    reshape x2 -> x0, local copies, waits for them, and re-layouts: 2.6 us -> none  [the longest x1 1.31 us: on_device(): be.reshape(1, FF)]
  transfers between devices with their start and end apart: 4 -> 0, of which waited for: 1 -> 0; matrix products, arithmetic and copies ran while one was open for 3% -> 0% of each run, Pallas kernels for 0% -> 0%
where the time goes in v1:
time: 70.2 us; the launch traced here: 70 us
  Pallas kernels  67.3 us (96%)
  local copies, waits for them, and re-layouts  2.71 us (4%)
    pallas_call x1, Pallas kernels, on_device(): pl.pallas_call(block_kernel, out_shape=jax.ShapeDtypeStruct((32, 64, D),...  67.3 us
    unnamed x1, local copies, waits for them, and re-layouts  2.71 us

profile of v1, /device:TPU:1, one launch (start us, length us, event | category | flops | bytes accessed | tf_op | source)
XLA Modules:
  0.0 70.0 jit_solution(7794988706512819524)
XLA Ops:
  0.0 67.3 %shard_map.91 = bf16[32,64,384]{2,1,0:T(8,128)(2,1)} custom-call(bf16[32,64,384]{2,1,0:T(8,128)(2,1)} %tok.1, bf16[384,1536]{1,0:T(8,128)(2,1)} %we.1, f32[1536]{0:T(1024)} %be.1, f32[9,1536]{1,0:T(8,128)} %wd.1, f32[1536]{0:T(1024)} %bd.1, bf16[1536,384]{1,0:T(8,128)(2,1)} %wp.1, bf16[384,1152]{1,0:T(8,128)(2,1)} %wqkv.1, bf16[384,384]{1,0:T(8,128)(2,1)} %wout.1, ...), custom_call_target="tpu_custom_call" | custom-call | tf_op jit(solution)/shard_map/pallas_call | solution.py:419
  67.3 2.7 %copy.11 = bf16[32,64,384]{2,1,0:T(8,128)(2,1)} copy(bf16[32,64,384]{2,1,0:T(8,128)(2,1)} %shard_map.91) | data formatting | bytes 3145728

commit v2 on v1

--- a/solution.py
+++ b/solution.py
@@ -100,13 +100,16 @@
         sides[:, sl] = twice_gelu(dot(cells, we[:, sl]) + be[:, sl]) * keep
 
 
-def place_sides(sides, grown):
+def place_sides(sides, grown, first, last):
     def step(y, _):
         grown[y + 1, 0, 0:1, :] = sides[pl.ds(y, 1), :]
         grown[y + 1, 9, 7:8, :] = sides[pl.ds(32 + y, 1), :]
         return 0
 
-    lax.fori_loop(0, 32, step, 0)
+    lax.fori_loop(first, last, step, 0)
+
+
+def place_corners(sides, grown):
     for r, at in ((0, 64), (33, 96)):
         grown[r, 0, 0:1, :] = sides[at + 15 : at + 16, :]
         grown[r, 9, 7:8, :] = sides[at + 16 : at + 17, :]
@@ -181,7 +184,7 @@
         vt[:, c * 256 : c * 256 + 256] = dot_of(wvt[...], x, NT).astype(BF)
 
 
-def attend_pair(qk, vt, bias, ctx, at):
+def attend_pairs(qk, vt, bias, ctx, places):
     row = iota((256, 128), 0)
     lane = iota((256, 128), 1)
     head_mask = one_hot(row // 64 == lane // 32)
@@ -191,7 +194,9 @@
     none = jnp.zeros((64, 128), BF)
     nothing = jnp.zeros((32, 128), BF)
     scale = LOG2E / math.sqrt(32.0)
-    for b in range(3):
+    units = [(at, b) for at in places for b in range(3)]
+    all_scores = []
+    for at, b in units:
         q = qk[pl.ds(at, 128), b * 128 : b * 128 + 128]
         k = qk[pl.ds(at, 128), D + b * 128 : D + b * 128 + 128]
         spread_k = jnp.concatenate(
@@ -205,7 +210,9 @@
             ],
             axis=0,
         )
-        scores = dot_of(spread_k, spread_q, NT)
+        all_scores.append(dot_of(spread_k, spread_q, NT))
+    softmaxes = []
+    for (at, b), scores in zip(units, all_scores):
         weights, inverse = [], []
         for h in range(4):
             s = scores[h * 64 : h * 64 + 64] * scale + bias[b * 4 + h]
@@ -213,7 +220,8 @@
             total = jnp.sum(w, axis=0, keepdims=True)
             inverse.append(jnp.broadcast_to(1.0 / total, (32, 128)))
             weights.append(w.astype(BF))
-        weights = jnp.concatenate(weights, axis=0)
+        softmaxes.append((jnp.concatenate(weights, axis=0), jnp.concatenate(inverse, axis=0)))
+    for (at, b), (weights, inverse) in zip(units, softmaxes):
         x = vt[b * 128 : b * 128 + 128, pl.ds(at, 128)]
         y = jnp.concatenate([x[:, 64:], x[:, :64]], axis=1)
         rows = []
@@ -223,8 +231,7 @@
             rows.append(jnp.concatenate([nothing, first[64:96] * lo], axis=1))
             rows.append(jnp.concatenate([nothing, second[96:128] * hi], axis=1))
         both = dot(jnp.concatenate(rows, axis=0), weights)
-        mine = jnp.where(low_lanes, both[:128], both[128:])
-        mine = mine * jnp.concatenate(inverse, axis=0)
+        mine = jnp.where(low_lanes, both[:128], both[128:]) * inverse
         ctx[b * 128 : b * 128 + 128, pl.ds(at, 128)] = mine.astype(BF)
 
 
@@ -260,14 +267,22 @@
 
 
 def block_kernel(
-    tok, we, be, wd, bd, wp, wqkv, wout, pos, out,
+    tok_at, we_at, be_at, wd_at, bd_at, wp_at, wqkv_at, wout_at, pos_at, out,
+    tok, we, be, wd, bd, wp, wqkv, wout, pos,
     perm, edges, halo, grown, sides, taps, flat, mb, landed, leaving, back,
     shifts, bias, wvt, grouped, normed, qk, vt, ctx,
-    halo_send, halo_recv, go_send, go_recv, back_send, back_recv,
+    load_sem, halo_send, halo_recv, go_send, go_recv, back_send, back_recv, out_sem,
 ):
     row, col = lax.axis_index("row"), lax.axis_index("col")
     core, x, y, z = place()
     me = slot(x, y, z)
+    pairs = [
+        (tok_at, tok), (we_at, we), (be_at, be), (pos_at, pos), (wqkv_at, wqkv),
+        (wd_at, wd), (bd_at, bd), (wp_at, wp), (wout_at, wout),
+    ]
+    loads = [pltpu.make_async_copy(a, b, load_sem.at[n]) for n, (a, b) in enumerate(pairs)]
+    for load in loads:
+        load.start()
 
     def beside(dr, dc):
         return (row + dr) % 16, (col + dc) % 8
@@ -281,11 +296,8 @@
         pl.semaphore_signal(barrier, inc=1, device_id=to, device_id_type=MESH)
 
     swap = swap_8x8()
+    loads[0].wait()
     permute_rows(tok, swap, perm, edges)
-    for k in range(12):
-        sl = slice(k * 128, k * 128 + 128)
-        flat[0:1, sl] = be[sl].reshape(1, 128)
-        flat[1:2, sl] = bd[sl].reshape(1, 128)
     pl.semaphore_wait(barrier, 69)
 
     rims = [
@@ -303,18 +315,23 @@
             src, dst, halo_send, halo_recv, device_id=beside(dr, dc), device_id_type=MESH
         ).start()
 
+    for n in range(1, 9):
+        loads[n].wait()
+    for k in range(12):
+        sl = slice(k * 128, k * 128 + 128)
+        flat[0:1, sl] = be[sl].reshape(1, 128)
+        flat[1:2, sl] = bd[sl].reshape(1, 128)
     set_taps(wd, flat.at[1:2], taps)
+    build_bias(pos, shifts, bias)
+    eye = one_hot(iota((D, D), 0) == iota((D, D), 1))
+    wvt[...] = dot_of(eye, wqkv[:, 768:], NT).astype(BF)
     bias_row = flat.at[0:1]
 
     def grow(c, _):
         expand_rows(perm, we, bias_row, grown, c * 4 + 1, 4)
         return 0
 
-    lax.fori_loop(0, 8, grow, 0)
-    build_bias(pos, shifts, bias)
-    eye = one_hot(iota((D, D), 0) == iota((D, D), 1))
-    wvt[...] = dot_of(eye, wqkv[:, 768:], NT).astype(BF)
-
+    lax.fori_loop(0, 5, grow, 0)
     pltpu.make_async_copy(halo, halo, halo_recv).wait()
     ends = dot(swap[:128, :128], halo[0:128, :]).astype(BF).reshape(2, 4, 16, D)
     perm[0] = ends[0]
@@ -331,11 +348,18 @@
         grown[33] = jnp.zeros(grown.shape[1:], F32)
 
     expand_sides(halo[128:256, :], we, bias_row, sides, row, col, 15, 7)
-    place_sides(sides, grown)
+    place_sides(sides, grown, 0, 20)
+    place_corners(sides, grown)
 
     def mix(n, _):
         h, m = n // 4, n % 4
-        k = (x + y + z + m) % 4
+
+        @pl.when(n == 4)
+        def _():
+            lax.fori_loop(5, 8, grow, 0)
+            place_sides(sides, grown, 20, 32)
+
+        k = (x + y + z + m + 1) % 4
         conv_project(perm, grown, taps, wp, mb, 16 * h + 4 * k)
         for dy, dz in [(b, c) for b in (2, 1, 3, 0) for c in (2, 1, 3, 0)]:
             Y, Z = (y + dy) % 4, (z + dz) % 4
@@ -351,9 +375,9 @@
             if (dy, dz) != (0, 0):
                 send()
             else:
-                pl.when(m != 0)(send)
-
-                @pl.when(m == 0)
+                pl.when(m != 3)(send)
+
+                @pl.when(m == 3)
                 def _():
                     pltpu.make_async_copy(piece, landed.at[h, me], go_recv.at[h]).start()
         return 0
@@ -369,11 +393,12 @@
             group_rows(here, swap16, grouped, normed, sb)
         project_qkv(normed, wqkv, wvt, qk, vt)
 
-        def pair(n, _):
-            attend_pair(qk, vt, bias, ctx, pl.multiple_of(n * 128, 128))
+        def four(n, _):
+            places = [pl.multiple_of(n * 512 + j * 128, 128) for j in range(4)]
+            attend_pairs(qk, vt, bias, ctx, places)
             return 0
 
-        lax.fori_loop(0, 8, pair, 0)
+        lax.fori_loop(0, 2, four, 0)
         project_out(ctx, wout, grouped)
         for sb in range(4):
             ungroup_rows(grouped, swap16, leaving.at[h], sb)
@@ -388,27 +413,32 @@
         return 0
 
     lax.fori_loop(0, 2, attend, 0)
-
+    pltpu.make_async_copy(halo, halo, halo_send).wait()
+
+    outs = []
     for h in range(2):
         here = back.at[16 * h : 16 * h + 16]
         pltpu.make_async_copy(here, here, back_recv.at[h]).wait()
-
-        def finish(c, _):
-            v = dot(swap, back[pl.ds(c * 4, 4)].reshape(256, D))
-            out[pl.ds(c * 4, 4)] = v.astype(BF).reshape(4, 64, D)
-            return 0
-
-        lax.fori_loop(4 * h, 4 * h + 4, finish, 0)
-    pltpu.make_async_copy(halo, halo, halo_send).wait()
+        for c in range(4 * h, 4 * h + 4):
+            v = dot(swap, back[c * 4 : c * 4 + 4].reshape(256, D))
+            tok[c * 4 : c * 4 + 4] = v.astype(BF).reshape(4, 64, D)
+            copy = pltpu.make_async_copy(
+                tok.at[c * 4 : c * 4 + 4], out.at[c * 4 : c * 4 + 4], out_sem.at[c]
+            )
+            copy.start()
+            outs.append(copy)
     for h in range(2):
         sent = landed.at[h, 0:63]
         pltpu.make_async_copy(sent, sent, go_send.at[h]).wait()
         pltpu.make_async_copy(sent, sent, back_send.at[h]).wait()
-
-
-def on_device(tokens, we, be, wd, bd, wp, wqkv, wout, pos):
-    vm = pl.BlockSpec(memory_space=pltpu.VMEM)
-    shapes = [
+    for copy in outs:
+        copy.wait()
+
+
+def on_device(*args):
+    anywhere = pl.BlockSpec(memory_space=pl.ANY)
+    shapes = [(a.shape, a.dtype) for a in args]
+    shapes += [
         ((34, 4, 16, D), BF), ((64, D), BF), ((256, D), BF), ((34, 10, 8, FF), F32),
         ((128, FF), F32), ((10, 8, FF), F32), ((8, FF), F32), ((32, 4, 16, D), BF),
         ((2, 64, 16, D), BF), ((2, 64, 16, D), BF), ((32, 4, 16, D), BF),
@@ -419,14 +449,14 @@
     return pl.pallas_call(
         block_kernel,
         out_shape=jax.ShapeDtypeStruct((32, 64, D), BF),
-        in_specs=[vm] * 9,
-        out_specs=vm,
+        in_specs=[anywhere] * 9,
+        out_specs=anywhere,
         scratch_shapes=[pltpu.VMEM(*s) for s in shapes]
-        + [dma, dma, dma((2,)), dma((2,)), dma((2,)), dma((2,))],
+        + [dma((9,)), dma, dma, dma((2,)), dma((2,)), dma((2,)), dma((2,)), dma((8,))],
         compiler_params=pltpu.CompilerParams(
             collective_id=0, has_side_effects=True, vmem_limit_bytes=58 << 20
         ),
-    )(tokens, we, be, wd, bd, wp, wqkv, wout, pos)
+    )(*args)
 
 
 def solution(mesh):

time: 70.2 us -> 64.5 us (0.919)
  Pallas kernels: 67.3 us -> 61.7 us
    pallas_call x1, Pallas kernels: 67.3 us -> 61.7 us  [on_device(): pl.pallas_call(block_kernel, out_shape=jax.ShapeDtypeStruct((32, 64, D),...]
where the time goes in v2:
time: 64.5 us; the launch traced here: 64.4 us
  Pallas kernels  61.7 us (96%)
  local copies, waits for them, and re-layouts  2.71 us (4%)
    pallas_call x1, Pallas kernels, on_device(): pl.pallas_call(block_kernel, out_shape=jax.ShapeDtypeStruct((32, 64, D),...  61.7 us
    unnamed x1, local copies, waits for them, and re-layouts  2.71 us

profile of v2, /device:TPU:1, one launch (start us, length us, event | category | flops | bytes accessed | tf_op | source)
XLA Modules:
  0.0 64.4 jit_solution(7168288300356944994)
XLA Ops:
  0.0 61.7 %shard_map.91 = bf16[32,64,384]{2,1,0:T(8,128)(2,1)} custom-call(bf16[32,64,384]{2,1,0:T(8,128)(2,1)} %tok_at.1, bf16[384,1536]{1,0:T(8,128)(2,1)} %we_at.1, f32[1536]{0:T(1024)} %be_at.1, f32[9,1536]{1,0:T(8,128)} %wd_at.1, f32[1536]{0:T(1024)} %bd_at.1, bf16[1536,384]{1,0:T(8,128)(2,1)} %wp_at.1, bf16[384,1152]{1,0:T(8,128)(2,1)} %wqkv_at.1, ...), custom_call_target="tpu_custom_call" | custom-call | tf_op jit(solution)/shard_map/pallas_call | solution.py:449
  61.7 2.7 %copy.11 = bf16[32,64,384]{2,1,0:T(8,128)(2,1)} copy(bf16[32,64,384]{2,1,0:T(8,128)(2,1)} %shard_map.91) | data formatting | bytes 3145728

commit v3 on v2

--- a/solution.py
+++ b/solution.py
@@ -66,13 +66,12 @@
 def permute_rows(tok, swap, perm, edges):
     r, n = iota((64, 256), 0), iota((64, 256), 1)
 
-    def step(c, total):
-        x = tok[pl.ds(c * 4, 4)].reshape(256, D)
-        perm[pl.ds(c * 4 + 1, 4)] = dot(swap, x).astype(BF).reshape(4, 4, 16, D)
-        pick = one_hot(n == (r % 32 - 4 * c) * 64 + (r // 32) * 63)
-        return total + dot(pick, x)
-
-    edges[...] = lax.fori_loop(0, 8, step, jnp.zeros((64, D), F32)).astype(BF)
+    total = jnp.zeros((64, D), F32)
+    for c in range(8):
+        x = tok[c * 4 : c * 4 + 4].reshape(256, D)
+        perm[c * 4 + 1 : c * 4 + 5] = dot(swap, x).astype(BF).reshape(4, 4, 16, D)
+        total = total + dot(one_hot(n == (r % 32 - 4 * c) * 64 + (r // 32) * 63), x)
+    edges[...] = total.astype(BF)
 
 
 def expand_rows(perm, we, be, grown, r0, n):
@@ -80,8 +79,9 @@
     for b in range(6):
         sl = slice(b * 256, b * 256 + 256)
         g = twice_gelu(dot(x, we[:, sl]) + be[:, sl]).reshape(n, 8, 8, 256)
-        grown[pl.ds(r0, n), 1:9, :, sl] = g
         for y in range(n):
+            for t in range(8):
+                grown[r0 + y, 1 + t, :, sl] = g[y, t]
             grown[r0 + y, 0, :, sl] = pltpu.roll(g[y, 7], 1, 0)
             grown[r0 + y, 9, :, sl] = pltpu.roll(g[y, 0], 7, 0)
 
@@ -249,16 +249,13 @@
 
 def place():
     row, col = lax.axis_index("row"), lax.axis_index("col")
-    x = (row // 8) * 2 + col // 4
-    return row % 2, x, (row // 2) % 4, col % 4
-
-
-def device(core, x, y, z):
-    return ((x // 2) * 8 + y * 2 + core, (x % 2) * 4 + z)
-
-
-def slot(x, y, z):
-    return ((x // 2) * 4 + y) * 8 + (x % 2) * 4 + z
+    x = lax.div(row, 8) * 2 + lax.div(col, 4)
+    return lax.rem(row, 2), x, lax.rem(lax.div(row, 2), 4), lax.rem(col, 4)
+
+
+def along_x(x):
+    high, low = lax.div(x, 2), lax.rem(x, 2)
+    return high * 8, low * 4, high * 32 + low * 4
 
 
 ORDER = [(a, b, c) for a in (2, 1, 3, 0) for b in (2, 1, 3, 0) for c in (2, 1, 3, 0)]
@@ -275,7 +272,16 @@
 ):
     row, col = lax.axis_index("row"), lax.axis_index("col")
     core, x, y, z = place()
-    me = slot(x, y, z)
+    xs = [along_x(lax.rem(x + d, 4)) for d in range(4)]
+    ys = [lax.rem(y + d, 4) for d in range(4)]
+    zs = [lax.rem(z + d, 4) for d in range(4)]
+    rows_of = [2 * a + core for a in ys]
+    slots_of = [8 * a for a in ys]
+    me = xs[0][2] + 8 * y + z
+
+    def offset_device(dx, dy, dz):
+        return xs[dx][0] + rows_of[dy], xs[dx][1] + zs[dz]
+
     pairs = [
         (tok_at, tok), (we_at, we), (be_at, be), (pos_at, pos), (wqkv_at, wqkv),
         (wd_at, wd), (bd_at, bd), (wp_at, wp), (wout_at, wout),
@@ -285,14 +291,14 @@
         load.start()
 
     def beside(dr, dc):
-        return (row + dr) % 16, (col + dc) % 8
+        return lax.rem(row + dr + 16, 16), lax.rem(col + dc + 8, 8)
 
     barrier = pltpu.get_barrier_semaphore()
     for dr, dc in NEAR:
         if dr != 0:
             pl.semaphore_signal(barrier, inc=1, device_id=beside(dr, dc), device_id_type=MESH)
     for dx, dy, dz in OFFSETS:
-        to = device(core, (x + dx) % 4, (y + dy) % 4, (z + dz) % 4)
+        to = offset_device(dx, dy, dz)
         pl.semaphore_signal(barrier, inc=1, device_id=to, device_id_type=MESH)
 
     swap = swap_8x8()
@@ -327,11 +333,8 @@
     wvt[...] = dot_of(eye, wqkv[:, 768:], NT).astype(BF)
     bias_row = flat.at[0:1]
 
-    def grow(c, _):
-        expand_rows(perm, we, bias_row, grown, c * 4 + 1, 4)
-        return 0
-
-    lax.fori_loop(0, 5, grow, 0)
+    expand_rows(perm, we, bias_row, grown, 1, 16)
+    expand_rows(perm, we, bias_row, grown, 17, 4)
     pltpu.make_async_copy(halo, halo, halo_recv).wait()
     ends = dot(swap[:128, :128], halo[0:128, :]).astype(BF).reshape(2, 4, 16, D)
     perm[0] = ends[0]
@@ -352,24 +355,25 @@
     place_corners(sides, grown)
 
     def mix(n, _):
-        h, m = n // 4, n % 4
+        h, m = lax.div(n, 4), lax.rem(n, 4)
 
         @pl.when(n == 4)
         def _():
-            lax.fori_loop(5, 8, grow, 0)
+            expand_rows(perm, we, bias_row, grown, 21, 12)
             place_sides(sides, grown, 20, 32)
 
-        k = (x + y + z + m + 1) % 4
-        conv_project(perm, grown, taps, wp, mb, 16 * h + 4 * k)
+        first = 16 * h + 4 * lax.rem(x + y + z + m + 1, 4)
+        conv_project(perm, grown, taps, wp, mb, first)
+        targets = [along_x(lax.rem(x + m + 5 - d, 4)) for d in range(4)]
         for dy, dz in [(b, c) for b in (2, 1, 3, 0) for c in (2, 1, 3, 0)]:
-            Y, Z = (y + dy) % 4, (z + dz) % 4
-            X = (k - Y - Z + 8) % 4
-            piece = mb.at[16 * h + 4 * k + Y, Z]
+            X = targets[(dy + dz) % 4]
+            piece = mb.at[first + ys[dy], zs[dz]]
+            to = (X[0] + rows_of[dy], X[1] + zs[dz])
 
             def send():
                 pltpu.make_async_remote_copy(
                     piece, landed.at[h, me], go_send.at[h], go_recv.at[h],
-                    device_id=device(core, X, Y, Z), device_id_type=MESH,
+                    device_id=to, device_id_type=MESH,
                 ).start()
 
             if (dy, dz) != (0, 0):
@@ -402,12 +406,12 @@
         project_out(ctx, wout, grouped)
         for sb in range(4):
             ungroup_rows(grouped, swap16, leaving.at[h], sb)
-        mine = back.at[16 * h + 4 * ((x + y + z) % 4) + y, z]
+        mine = back.at[16 * h + 4 * lax.rem(x + y + z, 4) + y, z]
         for dx, dy, dz in OFFSETS:
-            X, Y, Z = (x + dx) % 4, (y + dy) % 4, (z + dz) % 4
+            theirs = xs[dx][2] + slots_of[dy] + zs[dz]
             pltpu.make_async_remote_copy(
-                leaving.at[h, slot(X, Y, Z)], mine, back_send.at[h], back_recv.at[h],
-                device_id=device(core, X, Y, Z), device_id_type=MESH,
+                leaving.at[h, theirs], mine, back_send.at[h], back_recv.at[h],
+                device_id=offset_device(dx, dy, dz), device_id_type=MESH,
             ).start()
         pltpu.make_async_copy(leaving.at[h, me], mine, back_recv.at[h]).start()
         return 0

time: 64.5 us -> 64.3 us (level)
  no operation moved by 1% of the time
where the time goes in v3:
time: 64.3 us; the launch traced here: 64.2 us
  Pallas kernels  61.4 us (95%)
  local copies, waits for them, and re-layouts  2.71 us (4%)
    pallas_call x1, Pallas kernels, on_device(): pl.pallas_call(block_kernel, out_shape=jax.ShapeDtypeStruct((32, 64, D),...  61.4 us
    unnamed x1, local copies, waits for them, and re-layouts  2.71 us

profile of v3, /device:TPU:1, one launch (start us, length us, event | category | flops | bytes accessed | tf_op | source)
XLA Modules:
  0.0 64.2 jit_solution(6344309735944792073)
XLA Ops:
  0.0 61.4 %shard_map.91 = bf16[32,64,384]{2,1,0:T(8,128)(2,1)} custom-call(bf16[32,64,384]{2,1,0:T(8,128)(2,1)} %tok_at.1, bf16[384,1536]{1,0:T(8,128)(2,1)} %we_at.1, f32[1536]{0:T(1024)} %be_at.1, f32[9,1536]{1,0:T(8,128)} %wd_at.1, f32[1536]{0:T(1024)} %bd_at.1, bf16[1536,384]{1,0:T(8,128)(2,1)} %wp_at.1, bf16[384,1152]{1,0:T(8,128)(2,1)} %wqkv_at.1, ...), custom_call_target="tpu_custom_call" | custom-call | tf_op jit(solution)/shard_map/pallas_call | solution.py:453
  61.4 2.7 %copy.11 = bf16[32,64,384]{2,1,0:T(8,128)(2,1)} copy(bf16[32,64,384]{2,1,0:T(8,128)(2,1)} %shard_map.91) | data formatting | bytes 3145728
